TPU v7x, 512 devices: a whole 4x8x8 slice. The times are simulated.
512 devices in a mesh: cell: 8 (over z), donor: 8 (over x, core), gene: 8 (over y).
Axes of the slice: x: 4, y: 8, z: 8, core: 2. Of those that a mesh axis runs over, the one named last changes fastest.
Arguments:
- counts: int32 [32768, 2048], P(('cell', 'donor'), 'gene'), may hold values from 0 to 35
- cell_donor: int32 [32768], P(('cell', 'donor')), may hold values from 0 to 511, as said below
- cell_type: int32 [32768], P(('cell', 'donor')), may hold values from -1 to 23, as said below
- covariates: float32 [512, 50], P(('cell', 'donor')), may hold values from -6 to 6
- dosage: int32 [8192, 512], P('gene'), may hold values from 0 to 2
- windows: int32 [2048, 1024], P(('gene', 'cell', 'donor')), may hold values from -1 to 8191, as said below
Outputs:
- association: float32 [24, 2048, 1024], P(None, ('gene', 'cell', 'donor'))
Inputs may be any that keep to these rules, and one draw needn't show every extreme that they name: `cell_donor`: rows come in blocks of 512: a row of block b names a donor d with (d // 8) % 8 = b % 8. Every donor has at least one cell of every cell type. `cell_type`: in each block of 512 rows the live slots (type 0 or more) come first and the empty ones (-1) last; the number of live slots varies from block to block and some block is full. `windows`: row j lists consecutive SNP numbers in ascending order, then -1 to its end; all of them lie in [b * 1024, (b + 1) * 1024) with b = j // 256. A window holds 512 to 1024 SNPs, some window holds exactly 1024, and the last gene's window ends at the last SNP.
All inputs are finite; a program needn't handle non-finite values.
Results may differ from a plain program's by a relative error of at most 0.00045.
Values sent between devices are 32-bit elements; how exact they have to be, the bound alone decides.
No kernel may reach another device: no remote copies, remote signals or barrier semaphores. Data moves between devices by JAX's collectives and lax.ppermute only.
A program may use at most 64 MiB of HBM per device.

v0:
```python
import math
import jax
import jax.numpy as jnp
from jax import lax
from jax.sharding import PartitionSpec as P

CT = 24


def log_cpm(pseudobulk, library):
    return jnp.log2((pseudobulk + 0.5) / (library + 1.0) * 1000000.0)


def with_intercept(covariates):
    intercept = jnp.ones((covariates.shape[0], 1), jnp.float32)
    return jnp.concatenate([intercept, covariates], axis=1)


def factor_lower(gram_sum):
    order = gram_sum.shape[0]
    factor = jnp.zeros_like(gram_sum)
    for column in range(order):
        known = factor[column, :column]
        pivot = jnp.sqrt(gram_sum[column, column] - jnp.sum(known * known))
        factor = factor.at[column, column].set(pivot)
        if column + 1 < order:
            below = gram_sum[column + 1 :, column] - jnp.dot(
                factor[column + 1 :, :column], known, precision=lax.Precision.HIGHEST
            )
            factor = factor.at[column + 1 :, column].set(below / pivot)
    return factor


def solve_written(factor, right_rows):
    order = factor.shape[0]
    forward = []
    for row in range(order):
        value = right_rows[row]
        if row > 0:
            value = value - jnp.dot(
                factor[row, :row], jnp.stack(forward), precision=lax.Precision.HIGHEST
            )
        forward.append(value / factor[row, row])
    backward = [None] * order
    for row in range(order - 1, -1, -1):
        value = forward[row]
        if row < order - 1:
            later = jnp.stack(backward[row + 1 :])
            value = value - jnp.dot(factor[row + 1 :, row], later, precision=lax.Precision.HIGHEST)
        backward[row] = value / factor[row, row]
    return jnp.stack(backward)


def solve_normal(gram_sum, cross_sum):
    order = gram_sum.shape[0]
    factor = factor_lower(gram_sum)
    inverse = solve_written(factor, jnp.eye(order, dtype=jnp.float32))
    return jnp.einsum("kj,cjg->ckg", inverse, cross_sum, precision=lax.Precision.HIGHEST)


def association_block(residual, dosage, windows, first_snp):
    window_len = windows.shape[1]
    every_snp = jnp.einsum(
        "sd,dcg->gsc", dosage.astype(jnp.float32), residual, precision=lax.Precision.HIGHEST
    )
    padded = jnp.pad(every_snp, ((0, 0), (0, window_len), (0, 0)))
    starts = windows[:, 0] - first_snp
    gene_ids = jnp.arange(windows.shape[0], dtype=jnp.int32)

    def one_gene(pair):
        gene_id, start = pair
        gene_rows = lax.dynamic_index_in_dim(padded, gene_id, 0, keepdims=False)
        return lax.dynamic_slice_in_dim(gene_rows, start, window_len, 0)

    sliced = lax.map(one_gene, (gene_ids, starts))
    products = jnp.transpose(sliced, (2, 0, 1))
    scaling = 1.0 / math.sqrt(dosage.shape[1])
    return jnp.where((windows >= 0)[None], products, 0.0) * scaling


def owner_index(cell_donor, cell_type, donors_here, groups):
    cell_slot = cell_donor // (donors_here * groups)
    local_donor = cell_slot * donors_here + cell_donor % donors_here
    return jnp.where(cell_type >= 0, local_donor * CT + cell_type, -1)


def per_device(counts, cell_donor, cell_type, covariates, dosage, windows):
    groups = lax.axis_size("donor")
    donors_here = covariates.shape[0]
    cell_count = counts.shape[0]
    owner_slot = owner_index(cell_donor, cell_type, donors_here, groups)
    counts_half = counts.astype(jnp.bfloat16)
    first_snp = lax.axis_index("gene") * dosage.shape[0]
    row_ids = lax.broadcasted_iota(
        jnp.int32, (donors_here * CT * lax.axis_size("cell"), cell_count), 0
    )
    onehot_table = (row_ids == owner_slot[None, :]).astype(jnp.bfloat16)
    pseudobulk = lax.psum_scatter(
        jnp.dot(onehot_table, counts_half, preferred_element_type=jnp.float32),
        "cell",
        scatter_dimension=0,
        tiled=True,
    )
    library = lax.psum(jnp.sum(pseudobulk, axis=1), "gene")
    expression = log_cpm(pseudobulk, library[:, None]).reshape(donors_here, CT, -1)
    design = with_intercept(covariates)
    gram_part = jnp.dot(design.T, design, precision=lax.Precision.HIGHEST)
    cross_part = jnp.einsum("dk,dcg->ckg", design, expression, precision=lax.Precision.HIGHEST)
    gram_sum, cross_sum = lax.psum((gram_part, cross_part), ("cell", "donor"))
    coefficients = solve_normal(gram_sum, cross_sum)
    residual = expression - jnp.einsum(
        "dk,ckg->dcg", design, coefficients, precision=lax.Precision.HIGHEST
    )
    regrouped = lax.all_to_all(residual, ("cell", "donor"), split_axis=2, concat_axis=0, tiled=True)
    return association_block(regrouped, dosage, windows, first_snp)


def solution(mesh):
    in_specs = (
        P(("cell", "donor"), "gene"),
        P(("cell", "donor")),
        P(("cell", "donor")),
        P(("cell", "donor"), None),
        P("gene", None),
        P(("gene", "cell", "donor"), None),
    )
    out_specs = P(None, ("gene", "cell", "donor"), None)
    return jax.shard_map(
        per_device, mesh=mesh, in_specs=in_specs, out_specs=out_specs, check_vma=False
    )
```

profile of v0, /device:TPU:1, one launch (start us, length us, event | category | flops | bytes accessed | tf_op | source)
XLA Modules:
  0.0 813.1 jit_solution(3078640551746485459)
XLA Ops:
  7.3 2.8 fusion
  10.5 252.7 %psum.23 = f32[51,51]{1,0:T(8,128)S(1)} all-reduce(f32[51,51]{1,0:T(8,128)S(1)} %fusion.449), channel_id=1, replica_groups=mesh['cell'=8,'donor'=8,'gene'=8] {'cell','donor'}, use_global_device_ids=true, to_apply=%region_4.5 | all-reduce | flops 2601 | bytes 20808 | tf_op jit(solution)/shard_map/psum | solution.py:109
  375.8 11.7 %scatter.456 = f32[51,51]{1,0:T(8,128)S(1)} dynamic-update-slice(f32[51,51]{1,0:T(8,128)S(1)} %copy.362, f32[1,1]{1,0:T(1,128)} %bitcast.220, s32[]{:T(128)} %constant.2846.clone.1, s32[]{:T(128)} %constant.2846.clone.1) | dynamic-update-slice | bytes 12 | tf_op jit(solution)/shard_map/scatter | solution.py:25
  431.1 1.8 fusion.481
  433.7 0.8 fusion.357
  437.5 0.8 fusion.367
  439.1 0.8 fusion.213
  445.6 0.8 fusion.221
  447.3 0.8 fusion.223
  448.2 0.8 fusion.224
  452.4 0.8 fusion.229
  456.7 0.8 fusion.234
  458.4 0.8 fusion.236
  463.5 0.8 fusion.242
  464.5 0.8 fusion.243
  467.2 0.8 fusion.246
  468.2 0.8 fusion.247
  478.6 0.8 fusion.379
  479.4 0.8 fusion.382
  481.9 0.8 fusion.257
  482.8 0.8 fusion.259
  487.5 0.8 fusion.271
  489.2 0.8 fusion.275
  493.4 0.8 fusion.285
  497.7 0.8 fusion.295
  498.6 0.8 fusion.297
  500.4 0.8 fusion.301
  508.7 0.8 fusion.317
  510.8 0.8 fusion.321
  517.2 1.0 reduce_sum.454
  518.2 14.1 %psum.21 = f32[192]{0:T(256)S(1)} all-reduce(f32[192]{0:T(256)S(1)} %reduce_sum.454), channel_id=1, replica_groups=mesh['cell'=8,'donor'=8,'gene'=8] {'gene'}, use_global_device_ids=true, to_apply=%region_2.3 | all-reduce | flops 192 | bytes 1536 | tf_op jit(solution)/shard_map/psum | solution.py:104
  532.3 1.0 log_multiply_fusion
  533.3 2.5 convolution_bitcast_fusion.1
  537.1 1.4 fusion.335
  539.7 193.4 %all-reduce.5.cloned.1.call-done = f32[24,51,256]{2,1,0:T(8,128)} async-done(((f32[24,51,256]{2,1,0:T(8,128)}), f32[24,51,256]{2,1,0:T(8,128)}) %all-reduce.5.cloned.1.call-update) | async-done | bytes 1253392 | tf_op jit(solution)/shard_map/psum | solution.py:109
  733.0 2.6 convolution_bitcast_fusion
  735.6 0.8 convolution_subtract_fusion
  736.9 1.5 reshape.3475
  738.4 9.8 %all-to-all-start = ((f32[64,1,768]{2,1,0:T(1,128)}), f32[64,1,768]{2,1,0:T(1,128)S(1)}, u32[]{:S(2)}, u32[]{:S(2)}) async-start(f32[64,1,768]{2,1,0:T(1,128)} %reshape.3475), calls=%async_computation.1 | async-start | bytes 393216 | tf_op jit(solution)/shard_map/all_to_all | solution.py:114
  748.3 11.7 %all-to-all-done = f32[64,1,768]{2,1,0:T(1,128)S(1)} async-done(((f32[64,1,768]{2,1,0:T(1,128)}), f32[64,1,768]{2,1,0:T(1,128)S(1)}, u32[]{:S(2)}, u32[]{:S(2)}) %all-to-all-start) | async-done | bytes 196640 | tf_op jit(solution)/shard_map/all_to_all | solution.py:114
  760.6 1.2 reduce.398
  762.6 6.8 fusion.5
  769.4 34.5 %while.115 = (s32[]{:T(128)}, f32[4,1024,24]{1,0,2:T(4,128)}, s32[4]{0:T(128)S(1)}, s32[4]{0:T(128)S(1)}, f32[4,2048,24]{1,2,0:T(8,128)S(1)}) while((s32[]{:T(128)}, f32[4,1024,24]{1,0,2:T(4,128)}, s32[4]{0:T(128)S(1)}, s32[4]{0:T(128)S(1)}, f32[4,2048,24]{1,2,0:T(8,128)S(1)}) %tuple.543), condition=%wide.region_55.56_spmd.clone, body=%wide.region_54.55_spmd.sunk.clone | while | flops 10 | bytes 590021 | solution.py:75
  775.1 2.9 dynamic_update_slice.10
  783.8 2.9 dynamic_update_slice.10
  792.4 2.9 dynamic_update_slice.10
  801.0 2.9 dynamic_update_slice.10
  803.9 1.9 multiply_bitcast_fusion
  (601 shorter events, 161.8 us)
Async XLA Ops:
  6.5 510.6 %reduce-scatter.2.cloned.1.call-start = ((), (), s32[]{:S(2)}) async-start(), calls=%async_computation.2 | async-start | bytes 1769472 | tf_op jit(solution)/shard_map/reduce_scatter | solution.py:98
  7.2 2.9 copy-start.1
  10.1 722.9 %all-reduce.5.cloned.1.call-start = ((), (), s32[]{:S(2)}) async-start(), calls=%async_computation.3 | async-start | bytes 2752512 | tf_op jit(solution)/shard_map/psum | solution.py:109
  736.4 11.7 %copy-start.2 = (s32[4,1024]{1,0:T(4,128)S(1)}, s32[4,1024]{1,0:T(4,128)}, u32[]{:S(2)}) copy-start(s32[4,1024]{1,0:T(4,128)} %param.215) | copy-start | bytes 49156
  736.9 25.7 %copy-start = (s32[1024,512]{1,0:T(8,128)S(1)}, s32[1024,512]{1,0:T(8,128)}, u32[]{:S(2)}) copy-start(s32[1024,512]{1,0:T(8,128)} %param.214) | copy-start | bytes 6291460
  738.4 21.7 %all-to-all-start = ((f32[64,1,768]{2,1,0:T(1,128)}), f32[64,1,768]{2,1,0:T(1,128)S(1)}, u32[]{:S(2)}, u32[]{:S(2)}) async-start(f32[64,1,768]{2,1,0:T(1,128)} %reshape.3475), calls=%async_computation.1 | async-start | bytes 393216 | tf_op jit(solution)/shard_map/all_to_all | solution.py:114
Sparse Core Ops, SparseCore 0:
  10.3 45.2 reduce-scatter.1
  535.9 197.0 all-reduce.4
where the time goes:
time: 824 us; the launch traced here: 813 us
  blocking collectives  267 us (32%)
  waiting for transfers between devices  205 us (25%)
  matrix products  96.3 us (12%)
  local copies, waits for them, and re-layouts  94.6 us (11%)
  between operations  84 us (10%)
  other arithmetic  39.8 us (5%)
  loops' own time  16.7 us (2%)
  starting transfers between devices  9.82 us (1%)
    psum x1, blocking collectives, per_device(): gram_sum, cross_sum = lax.psum((gram_part, cross_part), ('cell', 'donor'))  253 us
    psum x1, waiting for transfers between devices, per_device(): gram_sum, cross_sum = lax.psum((gram_part, cross_part), ('cell', 'donor'))  193 us
    dot_general x49, matrix products, solve_written(): jnp.dot(factor[row + 1:, row], later, precision=lax.Precision.HIGHEST)  37.7 us
    dot_general x49, matrix products, solve_written(): jnp.dot(factor[row, :row], jnp.stack(forward), precision=lax.Precision.HI...  36.4 us
    reduce_sum x49, other arithmetic, factor_lower(): pivot = jnp.sqrt(gram_sum[column, column] - jnp.sum(known * known))  30 us
    scatter x50, local copies, waits for them, and re-layouts, factor_lower(): factor = factor.at[column + 1:, column].set(below / pivot)  19.3 us
    scatter x50, local copies, waits for them, and re-layouts, factor_lower(): factor = factor.at[column, column].set(pivot)  18.7 us
    another operation x1, loops' own time, association_block(): sliced = lax.map(one_gene, (gene_ids, starts))  16.7 us
  transfers between devices with their start and end apart: 3, of which 2 were waited for; matrix products, arithmetic and copies ran while one was open for 23% of the time, Pallas kernels for 0%

commit v1 on v0

--- a/solution.py
+++ b/solution.py
@@ -1,3 +1,4 @@
+import functools
 import math
 import jax
 import jax.numpy as jnp
@@ -5,6 +6,14 @@
 from jax.sharding import PartitionSpec as P
 
 CT = 24
+
+
+def _name_set(inp, net_axis, axis_tag):
+    local_out = lax.psum(inp, axis_name=net_axis)
+    return lax.psum(local_out, axis_name=axis_tag)
+
+
+answer_outputs = functools.partial(_name_set, net_axis="cell", axis_tag="donor")
 
 
 def log_cpm(pseudobulk, library):
@@ -106,7 +115,7 @@
     design = with_intercept(covariates)
     gram_part = jnp.dot(design.T, design, precision=lax.Precision.HIGHEST)
     cross_part = jnp.einsum("dk,dcg->ckg", design, expression, precision=lax.Precision.HIGHEST)
-    gram_sum, cross_sum = lax.psum((gram_part, cross_part), ("cell", "donor"))
+    gram_sum, cross_sum = answer_outputs((gram_part, cross_part))
     coefficients = solve_normal(gram_sum, cross_sum)
     residual = expression - jnp.einsum(
         "dk,ckg->dcg", design, coefficients, precision=lax.Precision.HIGHEST

time: 824 us -> 570 us (0.69)
  blocking collectives: 267 us -> 72.3 us
  waiting for transfers between devices: 205 us -> 156 us
  local copies, waits for them, and re-layouts: 94.6 us -> 85.5 us
    psum x1 -> x2, blocking collectives: 253 us -> 57.9 us  [the longest x1 29.9 us: _name_set(): local_out = lax.psum(inp, axis_name=net_axis)]
    psum x1 -> x2, waiting for transfers between devices: 193 us -> 144 us  [the longest x1 73.7 us: _name_set(): return lax.psum(local_out, axis_name=axis_tag)]
    dynamic_update_slice x8, local copies, waits for them, and re-layouts: 12.1 us -> 3.65 us  [association_block(): sliced = lax.map(one_gene, (gene_ids, starts))]
  transfers between devices with their start and end apart: 3 -> 4, of which waited for: 2 -> 3; matrix products, arithmetic and copies ran while one was open for 23% -> 34% of each run, Pallas kernels for 0% -> 0%
where the time goes in v1:
time: 570 us; the launch traced here: 559 us
  waiting for transfers between devices  156 us (27%)
  matrix products  95.9 us (17%)
  local copies, waits for them, and re-layouts  85.5 us (15%)
  between operations  83.7 us (15%)
  blocking collectives  72.3 us (13%)
  other arithmetic  38.8 us (7%)
  loops' own time  15.7 us (3%)
  starting transfers between devices  11.4 us (2%)
    psum x1, waiting for transfers between devices, _name_set(): return lax.psum(local_out, axis_name=axis_tag)  73.7 us
    psum x1, waiting for transfers between devices, _name_set(): local_out = lax.psum(inp, axis_name=net_axis)  70.6 us
    dot_general x49, matrix products, solve_written(): jnp.dot(factor[row + 1:, row], later, precision=lax.Precision.HIGHEST)  37.5 us
    dot_general x49, matrix products, solve_written(): jnp.dot(factor[row, :row], jnp.stack(forward), precision=lax.Precision.HI...  36.3 us
    psum x1, blocking collectives, _name_set(): local_out = lax.psum(inp, axis_name=net_axis)  29.9 us
    reduce_sum x49, other arithmetic, factor_lower(): pivot = jnp.sqrt(gram_sum[column, column] - jnp.sum(known * known))  29.9 us
    psum x1, blocking collectives, _name_set(): return lax.psum(local_out, axis_name=axis_tag)  28 us
    scatter x50, local copies, waits for them, and re-layouts, factor_lower(): factor = factor.at[column + 1:, column].set(below / pivot)  19.3 us
  transfers between devices with their start and end apart: 4, of which 3 were waited for; matrix products, arithmetic and copies ran while one was open for 34% of the time, Pallas kernels for 0%

profile of v1, /device:TPU:1, one launch (start us, length us, event | category | flops | bytes accessed | tf_op | source)
XLA Modules:
  0.0 559.3 jit_solution(13609755686413058785)
XLA Ops:
  7.3 2.8 fusion
  10.5 29.9 %psum.38 = f32[51,51]{1,0:T(8,128)S(1)} all-reduce(f32[51,51]{1,0:T(8,128)S(1)} %fusion.449), channel_id=1, replica_groups=mesh['cell'=8,'donor'=8,'gene'=8] {'cell'}, use_global_device_ids=true, to_apply=%region_5.6 | all-reduce | flops 2601 | bytes 20808 | tf_op jit(solution)/shard_map/psum | solution.py:12
  40.4 28.0 %psum.39 = f32[51,51]{1,0:T(8,128)S(1)} all-reduce(f32[51,51]{1,0:T(8,128)S(1)} %psum.38), channel_id=1, replica_groups=mesh['cell'=8,'donor'=8,'gene'=8] {'donor'}, use_global_device_ids=true, to_apply=%region_6.7 | all-reduce | flops 2601 | bytes 20808 | tf_op jit(solution)/shard_map/psum | solution.py:13
  181.1 11.7 %scatter.456 = f32[51,51]{1,0:T(8,128)S(1)} dynamic-update-slice(f32[51,51]{1,0:T(8,128)S(1)} %copy.363, f32[1,1]{1,0:T(1,128)} %bitcast.220, s32[]{:T(128)} %constant.2846.clone.1, s32[]{:T(128)} %constant.2846.clone.1) | dynamic-update-slice | bytes 12 | tf_op jit(solution)/shard_map/scatter | solution.py:34
  235.3 1.8 fusion.481
  241.6 0.8 fusion.367
  248.0 0.8 fusion.219
  249.7 0.8 fusion.221
  250.6 0.8 fusion.222
  253.1 0.8 fusion.225
  254.8 0.8 fusion.227
  256.5 0.8 fusion.229
  261.5 0.8 fusion.235
  262.4 0.8 fusion.236
  265.1 0.8 fusion.239
  266.1 0.8 fusion.240
  273.9 0.8 fusion.249
  281.1 0.8 fusion.373
  288.1 0.8 fusion.263
  289.0 0.8 fusion.265
  291.5 0.8 fusion.271
  292.4 0.8 fusion.273
  297.3 0.8 fusion.285
  299.0 0.8 fusion.289
  301.0 0.8 fusion.293
  304.1 0.8 fusion.299
  305.2 0.8 fusion.301
  307.3 0.8 fusion.305
  315.0 1.0 reduce_sum.454
  316.0 14.3 %psum.35 = f32[192]{0:T(256)S(1)} all-reduce(f32[192]{0:T(256)S(1)} %reduce_sum.454), channel_id=1, replica_groups=mesh['cell'=8,'donor'=8,'gene'=8] {'gene'}, use_global_device_ids=true, to_apply=%region_2.3 | all-reduce | flops 192 | bytes 1536 | tf_op jit(solution)/shard_map/psum | solution.py:113
  330.4 1.0 log_multiply_fusion
  331.4 2.5 convolution_bitcast_fusion.1
  335.0 0.8 fusion.321
  341.3 70.6 %all-reduce.6.cloned.1.call-done = f32[24,51,256]{2,1,0:T(8,128)} async-done(((f32[24,51,256]{2,1,0:T(8,128)}), f32[24,51,256]{2,1,0:T(8,128)}) %all-reduce.6.cloned.1.call-update) | async-done | bytes 1253392 | tf_op jit(solution)/shard_map/psum | solution.py:12
  413.2 1.4 fusion.335
  415.8 73.7 %all-reduce.8.cloned.1.call-done = f32[24,51,256]{2,1,0:T(8,128)} async-done(((f32[24,51,256]{2,1,0:T(8,128)}), f32[24,51,256]{2,1,0:T(8,128)}) %all-reduce.8.cloned.1.call-update) | async-done | bytes 1253392 | tf_op jit(solution)/shard_map/psum | solution.py:13
  489.4 2.6 convolution_bitcast_fusion
  493.3 1.5 reshape.3475
  494.7 11.1 %all-to-all-start = ((f32[64,1,768]{2,1,0:T(1,128)}), f32[64,1,768]{2,1,0:T(1,128)S(1)}, u32[]{:S(2)}, u32[]{:S(2)}) async-start(f32[64,1,768]{2,1,0:T(1,128)} %reshape.3475), calls=%async_computation.1 | async-start | bytes 393216 | tf_op jit(solution)/shard_map/all_to_all | solution.py:123
  506.0 11.7 %all-to-all-done = f32[64,1,768]{2,1,0:T(1,128)S(1)} async-done(((f32[64,1,768]{2,1,0:T(1,128)}), f32[64,1,768]{2,1,0:T(1,128)S(1)}, u32[]{:S(2)}, u32[]{:S(2)}) %all-to-all-start) | async-done | bytes 196640 | tf_op jit(solution)/shard_map/all_to_all | solution.py:123
  518.4 1.1 reduce.398
  520.3 6.6 %fusion.5 = f32[4,1024,24]{1,2,0:T(8,128)S(1)} fusion(s32[1024,512]{1,0:T(8,128)S(1)} %copy-done, f32[64,8,24,4]{2,1,3,0:T(8,128)S(1)} %bitcast.2482), kind=kOutput, calls=%fused_computation.9 | convolution fusion | flops 604504064 | bytes 2686976 | tf_op jit(solution)/shard_map/sd,dcg->gsc/dot_general | solution.py:72
  527.0 24.4 %while.115 = (s32[]{:T(128)}, f32[4,1024,24]{1,0,2:T(4,128)S(1)}, s32[4]{0:T(128)S(1)}, s32[4]{0:T(128)S(1)}, f32[4,2048,24]{1,2,0:T(8,128)S(1)}) while((s32[]{:T(128)}, f32[4,1024,24]{1,0,2:T(4,128)S(1)}, s32[4]{0:T(128)S(1)}, s32[4]{0:T(128)S(1)}, f32[4,2048,24]{1,2,0:T(8,128)S(1)}) %tuple.552), condition=%wide.region_57.58_spmd.clone, body=%wide.region_56.57_spmd.sunk.clone | while | flops 10 | bytes 590021 | solution.py:84
  532.3 0.8 dynamic_update_slice.10
  538.4 0.8 dynamic_update_slice.10
  544.5 0.8 dynamic_update_slice.10
  550.6 0.8 dynamic_update_slice.10
  551.5 0.9 multiply_bitcast_fusion
  (607 shorter events, 162.7 us)
Async XLA Ops:
  6.5 308.5 %reduce-scatter.2.cloned.1.call-start = ((), (), s32[]{:S(2)}) async-start(), calls=%async_computation.2 | async-start | bytes 1769472 | tf_op jit(solution)/shard_map/reduce_scatter | solution.py:107
  7.2 2.9 copy-start.2
  10.1 401.8 %all-reduce.6.cloned.1.call-start = ((), (), s32[]{:S(2)}) async-start(), calls=%async_computation.3 | async-start | bytes 2752512 | tf_op jit(solution)/shard_map/psum | solution.py:12
  333.9 155.5 %all-reduce.8.cloned.1.call-start = ((), (), s32[]{:S(2)}) async-start(), calls=%async_computation.4 | async-start | bytes 2752512 | tf_op jit(solution)/shard_map/psum | solution.py:13
  492.8 13.1 %copy-start.3 = (s32[4,1024]{1,0:T(4,128)S(1)}, s32[4,1024]{1,0:T(4,128)}, u32[]{:S(2)}) copy-start(s32[4,1024]{1,0:T(4,128)} %param.215) | copy-start | bytes 49156
  493.3 27.0 %copy-start = (s32[1024,512]{1,0:T(8,128)S(1)}, s32[1024,512]{1,0:T(8,128)}, u32[]{:S(2)}) copy-start(s32[1024,512]{1,0:T(8,128)} %param.214) | copy-start | bytes 6291460
  494.7 23.0 %all-to-all-start = ((f32[64,1,768]{2,1,0:T(1,128)}), f32[64,1,768]{2,1,0:T(1,128)S(1)}, u32[]{:S(2)}, u32[]{:S(2)}) async-start(f32[64,1,768]{2,1,0:T(1,128)} %reshape.3475), calls=%async_computation.1 | async-start | bytes 393216 | tf_op jit(solution)/shard_map/all_to_all | solution.py:123
  520.3 6.7 %copy-start.1 = (f32[4,1024,24]{1,0,2:T(4,128)S(1)}, f32[4,1024,24]{1,0,2:T(4,128)}, u32[]{:S(2)}) copy-start(f32[4,1024,24]{1,0,2:T(4,128)} %custom-call) | copy-start | bytes 1179652
Sparse Core Ops, SparseCore 0:
  10.3 45.4 reduce-scatter.1
  334.0 77.8 all-reduce.5
  414.4 74.9 all-reduce.7
